TPU v7x, 32 devices: a whole 2x2x4 slice. The times are simulated.
32 devices in a mesh: dom: 8 (over z, y), sub: 4 (over x, core).
Axes of the slice: x: 2, y: 2, z: 4, core: 2. Of those that a mesh axis runs over, the one named last changes fastest.
Arguments:
- segments: float32 [64, 9, 128], P(('dom', 'sub')), may hold values from -6 to 6
- stress: float32 [3, 3], replicated, may hold values from -3 to 3
- drag_coef: float32 [64, 128], P(('dom', 'sub')), may hold values from 0.5 to 4
- send_ids: int32 [32, 8, 1], P(('dom', 'sub')), may hold values from -1 to 1, as said below
- partner_ids: int32 [32, 8, 1], P(('dom', 'sub')), may hold values from 0 to 1
Outputs:
- positions: float32 [64, 3, 128], P(('dom', 'sub'))
- velocity: float32 [64, 3, 128], P(('dom', 'sub'))
Inputs may be any that keep to these rules, and one draw needn't show every extreme that they name: `send_ids`: entry [d, p, s] names a block of device d, which goes in slot s to the device with dom index p and d's sub index; -1 marks an empty slot. Some device receives a block in every slot from every sender.
All inputs are finite; a program needn't handle non-finite values.
Results may differ from a plain program's by a relative error of at most 0.0003.
Values sent between devices are 32-bit elements; how exact they have to be, the bound alone decides.
A program may use at most 64 MiB of HBM per device.

v0:
```python
import math

import jax
import jax.numpy as jnp
from jax import lax
from jax.sharding import PartitionSpec as P

STEPS = 2


COUPLE = 0.0625
CORE_SQUARE = 0.5
TENSION = 0.25
STEP_LENGTH = 1.0
EPSILON = 1e-06


def pair_terms(target, source):
    offsets = [
        target[..., component, :][..., :, None] - source[..., component, :][..., None, :]
        for component in range(3)
    ]
    distance_sq = (
        CORE_SQUARE + offsets[0] * offsets[0] + offsets[1] * offsets[1] + offsets[2] * offsets[2]
    )
    inverse = lax.rsqrt(distance_sq)
    burgers_dot = target[..., 6, :][..., :, None] * source[..., 6, :][..., None, :]
    burgers_dot = burgers_dot + target[..., 7, :][..., :, None] * source[..., 7, :][..., None, :]
    burgers_dot = burgers_dot + target[..., 8, :][..., :, None] * source[..., 8, :][..., None, :]
    lines_dot = target[..., 3, :][..., :, None] * source[..., 3, :][..., None, :]
    lines_dot = lines_dot + target[..., 4, :][..., :, None] * source[..., 4, :][..., None, :]
    lines_dot = lines_dot + target[..., 5, :][..., :, None] * source[..., 5, :][..., None, :]
    weights = burgers_dot * lines_dot * inverse * inverse * inverse
    return (weights, offsets)


def force_on_target(weights, offsets):
    return jnp.stack([jnp.sum(weights * offset_c, axis=-1) for offset_c in offsets], axis=-2)


def external_force(stress, line_vec, burgers):
    pulled = [
        stress[component, 0] * burgers[:, 0]
        + stress[component, 1] * burgers[:, 1]
        + stress[component, 2] * burgers[:, 2]
        for component in range(3)
    ]
    first = pulled[1] * line_vec[:, 2] - pulled[2] * line_vec[:, 1]
    second = pulled[2] * line_vec[:, 0] - pulled[0] * line_vec[:, 2]
    third = pulled[0] * line_vec[:, 1] - pulled[1] * line_vec[:, 0]
    return jnp.stack([first, second, third], axis=1)


def chain_term(position):
    left_side = jnp.concatenate([position[..., :1], position[..., :-1]], axis=-1)
    right_side = jnp.concatenate([position[..., 1:], position[..., -1:]], axis=-1)
    return left_side + right_side - 2.0 * position


def group_forces(seg_state):
    block_count = seg_state.shape[0]
    seg_width = seg_state.shape[2]
    target = seg_state.transpose(1, 0, 2).reshape(9, block_count * seg_width)
    start_force = jnp.zeros((3, block_count * seg_width), jnp.float32)

    def add_block(accum_force, source):
        weights, offsets = pair_terms(target, source)
        return (accum_force + force_on_target(weights, offsets), None)

    running = lax.scan(
        add_block, start_force, lax.all_gather(seg_state, "sub", axis=0, tiled=True)
    )[0]
    return running.reshape(3, block_count, seg_width).transpose(1, 0, 2)


def target_side(pieces):
    weights, offsets = pair_terms(pieces[0], pieces[1])
    return force_on_target(weights, offsets)


def cross_forces(
    seg_state,
    send_list,
    is_valid,
    partner_list,
    send_table,
    peer_count,
    slot_count,
    full_send,
    kept_rows,
):
    block_count = seg_state.shape[0]
    seg_width = seg_state.shape[2]
    payload = jnp.where(is_valid[:, None, None], seg_state[jnp.maximum(send_list, 0)], 0.0)
    payload = payload.reshape(peer_count, slot_count, 9, seg_width)
    outgoing = payload if full_send else payload[:, :, 0:3]
    arrived, arrived_partner = (
        lax.all_to_all(outgoing, "dom", split_axis=0, concat_axis=0, tiled=True),
        lax.all_to_all(partner_list, "dom", split_axis=0, concat_axis=0, tiled=True),
    )
    if not full_send:
        arrived = jnp.concatenate([arrived, kept_rows[0]], axis=2)
    remote = arrived.reshape(-1, 9, seg_width)
    local_ids = arrived_partner.reshape(-1)
    local_blocks = seg_state[local_ids]
    item_count = remote.shape[0]
    batch_size = math.gcd(item_count, 16)
    local_batched = local_blocks.reshape(-1, batch_size, 9, seg_width)
    remote_batched = remote.reshape(-1, batch_size, 9, seg_width)
    back_kept = kept_rows[1]
    on_local = lax.map(target_side, (local_batched, remote_batched))
    going_back = local_blocks.reshape(peer_count, slot_count, 9, seg_width)
    going_back = going_back if full_send else going_back[:, :, 0:3]
    back_blocks = lax.all_to_all(going_back, "dom", split_axis=0, concat_axis=0, tiled=True)
    if not full_send:
        back_blocks = jnp.concatenate([back_blocks, kept_rows[1]], axis=2)
    back_kept = back_blocks[:, :, 3:9]
    own_batched = payload.reshape(-1, batch_size, 9, seg_width)
    back_batched = back_blocks.reshape(-1, batch_size, 9, seg_width)
    returned = lax.map(target_side, (own_batched, back_batched))
    block_range = jnp.arange(block_count, dtype=jnp.int32)
    local_table = (block_range[:, None] == local_ids[None, :]).astype(jnp.float32)
    add_local = jnp.einsum(
        "ni,icm->ncm",
        local_table,
        on_local.reshape(-1, 3, seg_width),
        precision=lax.Precision.HIGHEST,
    )
    add_sent = jnp.einsum(
        "ni,icm->ncm",
        send_table,
        returned.reshape(-1, 3, seg_width),
        precision=lax.Precision.HIGHEST,
    )
    return (add_local + add_sent, (arrived[:, :, 3:9], back_kept))


def local(segments, stress, drag_coef, send_ids, partner_ids):
    block_count = segments.shape[0]
    peer_count = send_ids.shape[1]
    slot_count = send_ids.shape[2]
    position = segments[:, 0:3]
    line_vec = segments[:, 3:6]
    burgers = segments[:, 6:9]
    applied = external_force(stress, line_vec, burgers)
    send_list = send_ids[0].reshape(-1)
    is_valid = send_list >= 0
    partner_list = partner_ids[0]
    block_range = jnp.arange(block_count, dtype=jnp.int32)
    send_table = (block_range[:, None] == send_list[None, :]).astype(jnp.float32)
    velocity = jnp.zeros_like(position)
    kept_rows = (None, None)
    for step_index in range(STEPS):
        full_send = step_index == 0
        seg_state = jnp.concatenate([position, line_vec, burgers], axis=1)
        grouped = group_forces(seg_state)
        crossed, kept_rows = cross_forces(
            seg_state,
            send_list,
            is_valid,
            partner_list,
            send_table,
            peer_count,
            slot_count,
            full_send,
            kept_rows,
        )
        force = COUPLE * (grouped + crossed) + applied + TENSION * chain_term(position)
        velocity = force / drag_coef[:, None, :]
        speed_sq = jnp.sum(velocity * velocity, axis=1)
        top_sq = lax.pmax(jnp.max(speed_sq), ("dom", "sub"))
        time_step = STEP_LENGTH / (jnp.sqrt(top_sq) + EPSILON)
        position = position + time_step * velocity
    return (position, velocity)


def solution(mesh):
    in_specs = (
        P(("dom", "sub"), None, None),
        P(),
        P(("dom", "sub"), None),
        P(("dom", "sub"), None, None),
        P(("dom", "sub"), None, None),
    )
    out_specs = (P(("dom", "sub"), None, None), P(("dom", "sub"), None, None))
    return jax.shard_map(local, mesh=mesh, in_specs=in_specs, out_specs=out_specs, check_vma=False)
```

profile of v0, /device:TPU:0, one launch (start us, length us, event | category | flops | bytes accessed | tf_op | source)
XLA Modules:
  0.0 170.0 jit_solution(14137370900399766309)
XLA Ops:
  0.6 0.6 copy-done.4
  1.3 0.7 copy.73
  2.0 7.3 %all-to-all-start = ((s32[8,1,1]{2,1,0:T(1,128)}), s32[8,1,1]{2,1,0:T(1,128)S(1)}, u32[]{:S(2)}, u32[]{:S(2)}) async-start(s32[8,1,1]{2,1,0:T(1,128)} %copy.73), calls=%async_computation | async-start | bytes 8192 | tf_op jit(solution)/shard_map/all_to_all | solution.py:99
  9.4 0.6 copy-done.6
  10.0 0.6 gather_fusion.1
  10.8 5.2 %all_gather.6 = f32[8,9,128]{2,1,0:T(8,128)S(1)} all-gather(f32[2,9,128]{2,1,0:T(8,128)S(1)} %copy.72), channel_id=1, replica_groups=mesh['dom'=8,'sub'=4] {'sub'}, dimensions={0}, use_global_device_ids=true | all-gather | bytes 46080 | tf_op jit(solution)/shard_map/all_gather | solution.py:71
  16.0 0.7 copy-done.2
  16.7 0.7 fusion.117
  17.4 0.6 copy.74
  18.0 5.1 %while.6 = (s32[]{:T(128)}, f32[3,256]{1,0:T(4,128)S(1)}, f32[9,256]{1,0:T(8,128)S(1)}, f32[8,9,128]{2,1,0:T(8,128)S(1)}, s32[]{:T(128)}, /*index=5*/s32[]{:T(12...) while((s32[]{:T(128)}, f32[3,256]{1,0:T(4,128)S(1)}, f32[9,256]{1,0:T(8,128)S(1)}, ...), condition=%wide.region_4.5_spmd.clone, body=%wide.region_0.4_spmd.clone.sunk | while | flops 952587 | bytes 54043 | solution.py:70
  18.7 0.5 fusion.126
  19.4 0.5 fusion.126
  20.0 0.5 fusion.126
  20.7 0.5 fusion.126
  21.3 0.5 fusion.126
  21.9 0.5 fusion.126
  22.6 0.5 fusion.126
  23.1 3.8 %multiply_subtract_fusion.2 = (f32[2,1,128]{2,0,1:T(2,128)S(1)}, f32[2,1,128]{2,0,1:T(2,128)S(1)}, f32[2,1,128]{2,0,1:T(2,128)S(1)}) fusion(f32[2,9,128]{2,0,1:T(2,128)S(1)} %copy-done, f32[]{:T(128)} %bitcast.59, f32[]{:T(128)} %bitcast.58, f32[]{:T(128)} %bitcast.57, f32[]{:T(128)} %bitcast.56, f32[]{:T(128)} %bitcast.55, f32[]{:T(128)} %bitcast.54), kind=kLoop, calls=%fused_computation.252 | loop fusion | flops 3328 | bytes 8216 | tf_op jit(solution)/shard_map/sub | solution.py:48
  26.9 1.9 %multiply_subtract_fusion.1 = (f32[2,1,128]{2,0,1:T(2,128)S(1)}, f32[2,1,128]{2,0,1:T(2,128)S(1)}) fusion(f32[2,1,128]{2,0,1:T(2,128)S(1)} %get-tuple-element.161, f32[2,9,128]{2,0,1:T(2,128)S(1)} %copy-done, f32[]{:T(128)} %bitcast.62, f32[]{:T(128)} %bitcast.61, f32[]{:T(128)} %bitcast.60), kind=kLoop, calls=%fused_computation.250 | loop fusion | flops 2048 | bytes 8204 | tf_op jit(solution)/shard_map/sub | solution.py:49
  28.9 6.0 %all-to-all-start.1 = ((f32[8,1,9,128]{3,1,2,0:T(1,128)}), f32[8,1,9,128]{3,1,2,0:T(1,128)S(1)}, u32[]{:S(2)}, u32[]{:S(2)}) async-start(f32[8,1,9,128]{3,1,2,0:T(1,128)} %copy.74), calls=%async_computation.1 | async-start | bytes 73728 | tf_op jit(solution)/shard_map/all_to_all | solution.py:98
  35.2 0.6 gather_fusion
  35.8 0.6 copy.76
  36.4 5.2 %all-to-all-done.1 = f32[8,1,9,128]{3,1,2,0:T(1,128)S(1)} async-done(((f32[8,1,9,128]{3,1,2,0:T(1,128)}), f32[8,1,9,128]{3,1,2,0:T(1,128)S(1)}, u32[]{:S(2)}, u32[]{:S(2)}) %all-to-all-start.1) | async-done | bytes 36896 | tf_op jit(solution)/shard_map/all_to_all | solution.py:98
  41.6 3.3 %all-to-all-start.2 = ((f32[8,1,9,128]{3,1,2,0:T(1,128)}), f32[8,1,9,128]{3,1,2,0:T(1,128)S(1)}, u32[]{:S(2)}, u32[]{:S(2)}) async-start(f32[8,1,9,128]{3,1,2,0:T(1,128)} %copy.76), calls=%async_computation.2 | async-start | bytes 73728 | tf_op jit(solution)/shard_map/all_to_all | solution.py:114
  45.0 2.2 %fusion.46 = (f32[8,128]{1,0:T(8,128)S(1)}, f32[8,128]{1,0:T(8,128)S(1)}, f32[8,128]{1,0:T(8,128)S(1)}) fusion(f32[8,128]{1,0:T(8,128)S(1)} %get-tuple-element.269, f32[8,128]{1,0:T(8,128)S(1)} %get-tuple-element.260, f32[8,128]{1,0:T(8,128)S(1)} %get-tuple-element.267, f32[8,128]{1,0:T(8,128)S(1)} %get-tuple-element.258, ...), kind=kLoop, calls=%fused_computation.114 | loop fusion | flops 3798016 | bytes 86016 | tf_op jit(solution)/shard_map/while/body/eval_jaxpr/reduce_sum | solution.py:38
  47.3 4.3 %all-to-all-done.2 = f32[8,1,9,128]{3,1,2,0:T(1,128)S(1)} async-done(((f32[8,1,9,128]{3,1,2,0:T(1,128)}), f32[8,1,9,128]{3,1,2,0:T(1,128)S(1)}, u32[]{:S(2)}, u32[]{:S(2)}) %all-to-all-start.2) | async-done | bytes 36896 | tf_op jit(solution)/shard_map/all_to_all | solution.py:114
  51.6 2.2 %fusion.53 = (f32[8,128]{1,0:T(8,128)S(1)}, f32[8,128]{1,0:T(8,128)S(1)}, f32[8,128]{1,0:T(8,128)S(1)}) fusion(f32[8,128]{1,0:T(8,128)S(1)} %get-tuple-element.251, f32[8,128]{1,0:T(8,128)S(1)} %get-tuple-element.242, f32[8,128]{1,0:T(8,128)S(1)} %get-tuple-element.249, f32[8,128]{1,0:T(8,128)S(1)} %get-tuple-element.240, ...), kind=kLoop, calls=%fused_computation.121 | loop fusion | flops 3798016 | bytes 86016 | tf_op jit(solution)/shard_map/while/body/eval_jaxpr/reduce_sum | solution.py:38
  53.8 0.7 copy-done.5
  54.6 0.6 reduce_max.18
  55.3 38.5 %pmax.14 = f32[]{:T(128)} all-reduce(f32[]{:T(128)} %reduce_max.18), channel_id=1, replica_groups=mesh['dom'=8,'sub'=4] {'dom','sub'}, use_global_device_ids=true, to_apply=%region_13.14 | all-reduce | flops 1 | bytes 8 | tf_op jit(solution)/shard_map/pmax | solution.py:171
  94.6 0.6 gather_fusion.3
  95.2 0.6 gather_fusion.2
  95.7 5.5 %all_gather.7 = f32[8,9,128]{2,1,0:T(8,128)S(1)} all-gather(f32[2,9,128]{2,1,0:T(8,128)S(1)} %get-tuple-element.276), channel_id=1, replica_groups=mesh['dom'=8,'sub'=4] {'sub'}, dimensions={0}, use_global_device_ids=true | all-gather | bytes 46080 | tf_op jit(solution)/shard_map/all_gather | solution.py:71
  101.4 0.6 copy.82
  102.0 4.5 %all-to-all-start.3 = ((f32[8,1,3,128]{3,1,2,0:T(1,128)}), f32[8,1,3,128]{3,1,2,0:T(1,128)S(1)}, u32[]{:S(2)}, u32[]{:S(2)}) async-start(f32[8,1,3,128]{3,1,2,0:T(1,128)} %copy.82), calls=%async_computation.3 | async-start | bytes 24576 | tf_op jit(solution)/shard_map/all_to_all | solution.py:98
  106.6 5.1 %while.7 = (s32[]{:T(128)}, f32[3,256]{1,0:T(4,128)S(1)}, f32[9,256]{1,0:T(8,128)S(1)}, f32[8,9,128]{2,1,0:T(8,128)S(1)}, s32[]{:T(128)}, /*index=5*/s32[]{:T(12...) while((s32[]{:T(128)}, f32[3,256]{1,0:T(4,128)S(1)}, f32[9,256]{1,0:T(8,128)S(1)}, ...), condition=%wide.region_18.19_spmd.clone, body=%wide.region_14.18_spmd.clone.sunk | while | flops 952587 | bytes 54043 | solution.py:70
  106.6 0.5 fusion.129
  107.3 0.5 fusion.129
  107.9 0.5 fusion.129
  111.8 0.6 copy.86
  112.4 0.6 all-to-all-done.3
  113.0 5.4 %all-to-all-start.4 = ((f32[8,1,3,128]{3,1,2,0:T(1,128)}), f32[8,1,3,128]{3,1,2,0:T(1,128)S(1)}, u32[]{:S(2)}, u32[]{:S(2)}) async-start(f32[8,1,3,128]{3,1,2,0:T(1,128)} %copy.86), calls=%async_computation.4 | async-start | bytes 24576 | tf_op jit(solution)/shard_map/all_to_all | solution.py:114
  118.4 6.5 %all-to-all-done.4 = f32[8,1,3,128]{3,1,2,0:T(1,128)S(1)} async-done(((f32[8,1,3,128]{3,1,2,0:T(1,128)}), f32[8,1,3,128]{3,1,2,0:T(1,128)S(1)}, u32[]{:S(2)}, u32[]{:S(2)}) %all-to-all-start.4) | async-done | bytes 12320 | tf_op jit(solution)/shard_map/all_to_all | solution.py:114
  125.0 2.2 %fusion.60 = (f32[8,128]{1,0:T(8,128)S(1)}, f32[8,128]{1,0:T(8,128)S(1)}, f32[8,128]{1,0:T(8,128)S(1)}) fusion(f32[8,128]{1,0:T(8,128)S(1)} %get-tuple-element.233, f32[8,128]{1,0:T(8,128)S(1)} %bitcast.356, f32[8,128]{1,0:T(8,128)S(1)} %get-tuple-element.231, f32[8,128]{1,0:T(8,128)S(1)} %bitcast.354, f32[8,128]{1,0:T(8,128)S(1)} %get-tuple-element.232, ...), kind=kLoop, calls=%fused_computation.128 | loop fusion | flops 3798016 | bytes 86016 | tf_op jit(solution)/shard_map/while/body/eval_jaxpr/reduce_sum | solution.py:38
  127.3 2.1 %fusion.67 = (f32[8,128]{1,0:T(8,128)S(1)}, f32[8,128]{1,0:T(8,128)S(1)}, f32[8,128]{1,0:T(8,128)S(1)}) fusion(f32[8,128]{1,0:T(8,128)S(1)} %get-tuple-element.224, f32[8,128]{1,0:T(8,128)S(1)} %get-tuple-element.215, f32[8,128]{1,0:T(8,128)S(1)} %get-tuple-element.222, f32[8,128]{1,0:T(8,128)S(1)} %get-tuple-element.213, ...), kind=kLoop, calls=%fused_computation.135 | loop fusion | flops 3798016 | bytes 86016 | tf_op jit(solution)/shard_map/while/body/eval_jaxpr/reduce_sum | solution.py:38
  129.6 0.6 reduce_max.19
  130.2 38.5 %pmax.15 = f32[]{:T(128)} all-reduce(f32[]{:T(128)} %reduce_max.19), channel_id=1, replica_groups=mesh['dom'=8,'sub'=4] {'dom','sub'}, use_global_device_ids=true, to_apply=%region_27.28 | all-reduce | flops 1 | bytes 8 | tf_op jit(solution)/shard_map/pmax | solution.py:171
  169.4 0.6 multiply_add_fusion
  (118 shorter events, 5.9 us)
Async XLA Ops:
  0.6 0.7 copy-start.4
  0.6 8.6 %copy-start = (f32[2,9,128]{2,0,1:T(2,128)S(1)}, f32[2,9,128]{2,0,1:T(2,128)}, u32[]{:S(2)}) copy-start(f32[2,9,128]{2,0,1:T(2,128)} %param.9) | copy-start | bytes 27652
  2.0 26.9 %all-to-all-start = ((s32[8,1,1]{2,1,0:T(1,128)}), s32[8,1,1]{2,1,0:T(1,128)S(1)}, u32[]{:S(2)}, u32[]{:S(2)}) async-start(s32[8,1,1]{2,1,0:T(1,128)} %copy.73), calls=%async_computation | async-start | bytes 8192 | tf_op jit(solution)/shard_map/all_to_all | solution.py:99
  9.3 0.7 copy-start.6
  16.0 0.7 copy-start.2
  28.9 12.7 %all-to-all-start.1 = ((f32[8,1,9,128]{3,1,2,0:T(1,128)}), f32[8,1,9,128]{3,1,2,0:T(1,128)S(1)}, u32[]{:S(2)}, u32[]{:S(2)}) async-start(f32[8,1,9,128]{3,1,2,0:T(1,128)} %copy.74), calls=%async_computation.1 | async-start | bytes 73728 | tf_op jit(solution)/shard_map/all_to_all | solution.py:98
  41.6 5.7 %copy-start.1 = (f32[8,1,9,128]{3,1,2,0:T(1,128)}, f32[8,1,9,128]{3,1,2,0:T(1,128)S(1)}, u32[]{:S(2)}) copy-start(f32[8,1,9,128]{3,1,2,0:T(1,128)S(1)} %all-to-all-done.1) | copy-start | bytes 110596
  41.6 10.0 %all-to-all-start.2 = ((f32[8,1,9,128]{3,1,2,0:T(1,128)}), f32[8,1,9,128]{3,1,2,0:T(1,128)S(1)}, u32[]{:S(2)}, u32[]{:S(2)}) async-start(f32[8,1,9,128]{3,1,2,0:T(1,128)} %copy.76), calls=%async_computation.2 | async-start | bytes 73728 | tf_op jit(solution)/shard_map/all_to_all | solution.py:114
  53.8 0.7 copy-start.5
  54.5 0.8 slice-start
  102.0 11.0 %all-to-all-start.3 = ((f32[8,1,3,128]{3,1,2,0:T(1,128)}), f32[8,1,3,128]{3,1,2,0:T(1,128)S(1)}, u32[]{:S(2)}, u32[]{:S(2)}) async-start(f32[8,1,3,128]{3,1,2,0:T(1,128)} %copy.82), calls=%async_computation.3 | async-start | bytes 24576 | tf_op jit(solution)/shard_map/all_to_all | solution.py:98
  113.0 11.9 %all-to-all-start.4 = ((f32[8,1,3,128]{3,1,2,0:T(1,128)}), f32[8,1,3,128]{3,1,2,0:T(1,128)S(1)}, u32[]{:S(2)}, u32[]{:S(2)}) async-start(f32[8,1,3,128]{3,1,2,0:T(1,128)} %copy.86), calls=%async_computation.4 | async-start | bytes 24576 | tf_op jit(solution)/shard_map/all_to_all | solution.py:114
  129.6 39.9 %copy-start.3 = (f32[2,3,128]{2,0,1:T(2,128)}, f32[2,3,128]{2,0,1:T(2,128)S(1)}, u32[]{:S(2)}) copy-start(f32[2,3,128]{2,0,1:T(2,128)S(1)} %get-tuple-element.297) | copy-start | bytes 9220
where the time goes:
time: 171 us; the launch traced here: 170 us
  blocking collectives  87.8 us (51%)
  starting transfers between devices  26.5 us (15%)
  other arithmetic  25.6 us (15%)
  waiting for transfers between devices  16.6 us (10%)
  local copies, waits for them, and re-layouts  10 us (6%)
  between operations  2.4 us (1%)
    pmax x2, blocking collectives, local(): top_sq = lax.pmax(jnp.max(speed_sq), ('dom', 'sub'))  77 us
    reduce_sum x20, other arithmetic, force_on_target(): jnp.sum(weights * offset_c, axis=-1)  17.2 us
    all_to_all x2, waiting for transfers between devices, cross_forces(): lax.all_to_all(going_back, 'dom', split_axis=0, concat_axis=0, tiled=True)  10.8 us
    all_gather x2, blocking collectives, group_forces(): lax.all_gather(seg_state, 'sub', axis=0, tiled=True)  10.7 us
    all_to_all x2, starting transfers between devices, cross_forces(): lax.all_to_all(outgoing, 'dom', split_axis=0, concat_axis=0, tiled=True)  10.5 us
    all_to_all x2, starting transfers between devices, cross_forces(): lax.all_to_all(going_back, 'dom', split_axis=0, concat_axis=0, tiled=True)  8.71 us
    all_to_all x1, starting transfers between devices, cross_forces(): lax.all_to_all(partner_list, 'dom', split_axis=0, concat_axis=0, tiled=True)  7.28 us
    all_to_all x2, waiting for transfers between devices, cross_forces(): lax.all_to_all(outgoing, 'dom', split_axis=0, concat_axis=0, tiled=True)  5.81 us
  transfers between devices with their start and end apart: 5, of which 4 were waited for; matrix products, arithmetic and copies ran while one was open for 13% of the time, Pallas kernels for 0%

commit v1 on v0

v1 whole, which is shorter than its diff:
```python
import functools

import jax
import jax.numpy as jnp
from jax import lax
from jax.experimental import pallas as pl
from jax.experimental.pallas import tpu as pltpu
from jax.sharding import PartitionSpec as P

STEPS = 2
COUPLE = 0.0625
CORE_SQUARE = 0.5
TENSION = 0.25
STEP_LENGTH = 1.0
EPSILON = 1e-06

MESH = pl.DeviceIdType.MESH
ROWS = 16
XROW, SROW, PROW = 9, 12, 13
UNROLL_LIMIT = 64


def repeat(first, last, body):
    if last - first <= UNROLL_LIMIT:
        for index in range(first, last):
            body(index)
    else:

        def step(index, carry):
            body(index)
            return carry

        lax.fori_loop(first, last, step, 0)


def kernel(
    n_dom,
    n_sub,
    seg_ref,
    drag_ref,
    stress_ref,
    send_ref,
    partner_ref,
    pos_ref,
    vel_ref,
    stage,
    held,
    numer,
    left_side,
    at_i,
    vel_i,
    acc,
    vel_tx,
    vel_rx,
    top1_tx,
    top1_rx,
    top2_tx,
    top2_rx,
    state_send,
    state_recv,
    vel_send,
    vel_recv,
    top1_send,
    top1_recv,
    top2_send,
    top2_recv,
):
    nb, _, width = seg_ref.shape
    slots = n_sub + n_dom - 1
    dom = lax.axis_index("dom")
    sub = lax.axis_index("sub")

    def sub_at(k):
        return (dom, lax.rem(sub + k, n_sub))

    def dom_at(k):
        return (lax.rem(dom + k, n_dom), sub)

    barrier = pltpu.get_barrier_semaphore()

    def greet_sub(k):
        pl.semaphore_signal(barrier, inc=1, device_id=sub_at(k), device_id_type=MESH)

    def greet_dom(k):
        pl.semaphore_signal(barrier, inc=1, device_id=dom_at(k), device_id_type=MESH)

    repeat(1, n_sub, greet_sub)
    repeat(1, n_dom, greet_dom)

    products = []
    for r in range(nb):
        burgers = seg_ref[r, 6:9, :]
        rows = [burgers[a : a + 1] * seg_ref[r, 3:6, :] for a in range(3)]
        block = jnp.concatenate(rows + [jnp.zeros((ROWS - 9, width), jnp.float32)], axis=0)
        products.append(block)
        held[0, r] = block
        held[0, r, XROW : XROW + 3, :] = seg_ref[r, 0:3, :]

    whole = [held[0, r] for r in range(nb)]
    row_id = lax.broadcasted_iota(jnp.int32, (ROWS, width), 0)

    def fill(q):
        sent = send_ref[0, q].astype(jnp.float32)
        partner = partner_ref[0, q].astype(jnp.float32)
        for r in range(nb):
            stage[q, r] = jnp.where(row_id == SROW, sent, jnp.where(row_id == PROW, partner, whole[r]))

    repeat(0, n_dom, fill)

    def sub_copy(k):
        return pltpu.make_async_remote_copy(
            src_ref=held.at[0],
            dst_ref=held.at[k],
            send_sem=state_send.at[k],
            recv_sem=state_recv.at[k],
            device_id=sub_at(k),
            device_id_type=MESH,
        )

    def dom_copy(k):
        slot = n_sub - 1 + k
        return pltpu.make_async_remote_copy(
            src_ref=stage.at[lax.rem(dom + k, n_dom)],
            dst_ref=held.at[slot],
            send_sem=state_send.at[slot],
            recv_sem=state_recv.at[slot],
            device_id=dom_at(k),
            device_id_type=MESH,
        )

    pl.semaphore_wait(barrier, slots - 1)
    repeat(1, n_dom, lambda k: dom_copy(k).start())
    repeat(1, n_sub, lambda k: sub_copy(k).start())

    applied_rows = []
    drag_rows = []
    for o in range(nb):
        b = [seg_ref[o, 6 + c : 7 + c, :] for c in range(3)]
        ln = [seg_ref[o, 3 + c : 4 + c, :] for c in range(3)]
        pulled = [
            stress_ref[c, 0] * b[0] + stress_ref[c, 1] * b[1] + stress_ref[c, 2] * b[2] for c in range(3)
        ]
        applied_rows.append(pulled[1] * ln[2] - pulled[2] * ln[1])
        applied_rows.append(pulled[2] * ln[0] - pulled[0] * ln[2])
        applied_rows.append(pulled[0] * ln[1] - pulled[1] * ln[0])
        drag_rows.extend([drag_ref[o : o + 1, :]] * 3)
    spare = 8 - 3 * nb
    zeros = jnp.zeros((spare, width), jnp.float32)
    applied = jnp.concatenate(applied_rows + [zeros], axis=0)
    drag = jnp.concatenate(drag_rows + [zeros + 1.0], axis=0)
    position = jnp.concatenate([seg_ref[o, 0:3, :] for o in range(nb)] + [zeros], axis=0)
    lane = lax.broadcasted_iota(jnp.int32, (8, width), 1)

    def split(value):
        high = value.astype(jnp.bfloat16)
        low = (value - high.astype(jnp.float32)).astype(jnp.bfloat16)
        return high, low

    for o in range(nb):
        high = products[o].astype(jnp.bfloat16).astype(jnp.float32)
        low = products[o] - high
        left_side[o] = jnp.concatenate([high, high, low], axis=0).T.astype(jnp.bfloat16)
        turned = whole[o].T
        for c in range(3):
            at_i[o, c] = jnp.broadcast_to(turned[:, XROW + c : XROW + c + 1], (width, width))

    def counts(slot, base, peer):
        table = []
        for o in range(nb):
            row = []
            for r in range(nb):
                value = jnp.full((1, width), base, jnp.float32)
                if peer is not None:
                    sent, partner = send_ref[0, peer], partner_ref[0, peer]
                    mine = jnp.logical_and(sent == o, partner == r)
                    value = value + jnp.where(mine, 1.0, 0.0)
                    source = stage if slot is None else held
                    place = dom if slot is None else slot
                    got, for_mine = source[place, 0, SROW : SROW + 1, :], source[place, 0, PROW : PROW + 1, :]
                    value = value + jnp.where(
                        jnp.logical_and(got == float(r), for_mine == float(o)), 1.0, 0.0
                    )
                row.append(value)
            table.append(row)
        return table

    def fill_numer(slot, base, peer):
        where = 0 if slot is None else slot
        table = counts(slot, base, peer)
        for o in range(nb):
            right = jnp.concatenate([held[where, r] * table[o][r] for r in range(nb)], axis=1)
            high, low = split(right)
            numer[where, o] = jnp.dot(
                left_side[o],
                jnp.concatenate([high, low, high], axis=0),
                preferred_element_type=jnp.float32,
            )

    def add_slot(slot, step, first=False):
        rows = []
        for r in range(nb):
            for c in range(3):
                row = held[slot, r, XROW + c : XROW + c + 1, :]
                if step is not None:
                    row = row + step * vel_rx[slot, r * 3 + c : r * 3 + c + 1, :]
                rows.append(jnp.broadcast_to(row, (8, width)))
        for o in range(nb):
            for g in range(width // 8):
                part = pl.ds(8 * g, 8)
                mine = [at_i[o, c, part, :] for c in range(3)]
                total = None if first else [acc[o, c, part, :] for c in range(3)]
                for r in range(nb):
                    off = [mine[c] - rows[r * 3 + c] for c in range(3)]
                    square = CORE_SQUARE + off[0] * off[0] + off[1] * off[1] + off[2] * off[2]
                    inverse = lax.rsqrt(square)
                    weight = numer[slot, o, part, pl.ds(width * r, width)] * inverse * (inverse * inverse)
                    terms = [weight * off[c] for c in range(3)]
                    total = terms if total is None else [total[c] + terms[c] for c in range(3)]
                for c in range(3):
                    acc[o, c, part, :] = total[c]

    def velocity_of(position):
        sums = []
        for o in range(nb):
            for c in range(3):
                sums.append(jnp.sum(acc[o, c].T, axis=0, keepdims=True))
        pair = jnp.concatenate(sums + [zeros], axis=0)
        before = jnp.where(lane == 0, position, pltpu.roll(position, 1, 1))
        after = jnp.where(lane == width - 1, position, pltpu.roll(position, width - 1, 1))
        chain = before + after - 2.0 * position
        force = COUPLE * pair + applied + TENSION * chain
        velocity = force / drag
        square = velocity * velocity
        tops = []
        for o in range(nb):
            tops.append(square[3 * o : 3 * o + 1] + square[3 * o + 1 : 3 * o + 2] + square[3 * o + 2 : 3 * o + 3])
        return velocity, functools.reduce(jnp.maximum, tops)

    def step_length(row):
        top = jnp.max(row, axis=1, keepdims=True)
        return STEP_LENGTH / (jnp.sqrt(top) + EPSILON)

    fill_numer(None, 1.0, dom)
    add_slot(0, None, first=True)

    def from_sub(k, carry):
        sub_copy(k).wait_recv()
        fill_numer(k, 1.0, None)
        add_slot(k, None)
        return carry

    def from_dom(k, carry):
        slot = n_sub - 1 + k
        dom_copy(k).wait_recv()
        fill_numer(slot, 0.0, lax.rem(dom - k + n_dom, n_dom))
        add_slot(slot, None)
        return carry

    lax.fori_loop(1, n_sub, from_sub, 0)
    lax.fori_loop(1, n_dom, from_dom, 0)
    velocity, top = velocity_of(position)
    vel_tx[...] = jnp.concatenate([velocity[0 : 3 * nb], top, zeros[: spare - 1]], axis=0)
    top1_tx[...] = top

    def vel_copy(slot, target):
        return pltpu.make_async_remote_copy(
            src_ref=vel_tx,
            dst_ref=vel_rx.at[slot],
            send_sem=vel_send,
            recv_sem=vel_recv,
            device_id=target,
            device_id_type=MESH,
        )

    def top1_copy(index):
        kd, ks = index // (n_sub - 1) + 1, index % (n_sub - 1) + 1
        return pltpu.make_async_remote_copy(
            src_ref=top1_tx,
            dst_ref=top1_rx.at[index],
            send_sem=top1_send,
            recv_sem=top1_recv,
            device_id=(lax.rem(dom + kd, n_dom), lax.rem(sub + ks, n_sub)),
            device_id_type=MESH,
        )

    others = (n_sub - 1) * (n_dom - 1)
    repeat(1, n_dom, lambda k: vel_copy(n_sub - 1 + k, dom_at(k)).start())
    repeat(0, others, lambda k: top1_copy(k).start())
    repeat(1, n_sub, lambda k: vel_copy(k, sub_at(k)).start())

    vel_rx[0] = vel_tx[...]
    turned = velocity.T
    for o in range(nb):
        for c in range(3):
            vel_i[o, c] = jnp.broadcast_to(turned[:, 3 * o + c : 3 * o + c + 1], (width, width))

    arrived = vel_rx.at[pl.ds(1, slots - 1)]
    pltpu.make_async_copy(arrived, arrived, vel_recv).wait()
    pltpu.make_async_copy(top1_rx, top1_rx, top1_recv).wait()
    near = jnp.max(vel_rx[:, 3 * nb : 3 * nb + 1, :], axis=0)
    far = jnp.max(top1_rx[...], axis=0)
    step = step_length(jnp.maximum(near, far))

    position = position + step * velocity
    for o in range(nb):
        for c in range(3):
            at_i[o, c] = at_i[o, c] + step * vel_i[o, c]
    add_slot(0, step, first=True)

    def again(slot, carry):
        add_slot(slot, carry)
        return carry

    lax.fori_loop(1, slots, again, step)
    velocity, top = velocity_of(position)
    top2_tx[...] = top

    def top2_copy(index):
        kd, ks = (index + 1) // n_sub, (index + 1) % n_sub
        return pltpu.make_async_remote_copy(
            src_ref=top2_tx,
            dst_ref=top2_rx.at[index],
            send_sem=top2_send,
            recv_sem=top2_recv,
            device_id=(lax.rem(dom + kd, n_dom), lax.rem(sub + ks, n_sub)),
            device_id_type=MESH,
        )

    repeat(0, n_sub * n_dom - 1, lambda k: top2_copy(k).start())
    for o in range(nb):
        vel_ref[o] = velocity[3 * o : 3 * o + 3]

    repeat(1, n_sub, lambda k: sub_copy(k).wait_send())
    repeat(1, n_dom, lambda k: dom_copy(k).wait_send())
    pltpu.make_async_copy(arrived, arrived, vel_send).wait()
    pltpu.make_async_copy(top1_rx, top1_rx, top1_send).wait()

    pltpu.make_async_copy(top2_rx, top2_rx, top2_recv).wait()
    step = step_length(jnp.maximum(jnp.max(top2_rx[...], axis=0), top))
    position = position + step * velocity
    for o in range(nb):
        pos_ref[o] = position[3 * o : 3 * o + 3]
    pltpu.make_async_copy(top2_rx, top2_rx, top2_send).wait()


def solution(mesh):
    n_dom, n_sub = mesh.shape["dom"], mesh.shape["sub"]

    def local(segments, stress, drag_coef, send_ids, partner_ids):
        nb, _, width = segments.shape
        slots = n_sub + n_dom - 1
        f32 = jnp.float32
        vmem = pl.BlockSpec(memory_space=pltpu.VMEM)
        smem = pl.BlockSpec(memory_space=pltpu.SMEM)
        out = jax.ShapeDtypeStruct((nb, 3, width), f32)
        words = slots * nb * width * nb * width + (n_dom + slots) * nb * ROWS * width + 9 * nb * width * width
        return pl.pallas_call(
            functools.partial(kernel, n_dom, n_sub),
            out_shape=(out, out),
            in_specs=[vmem, vmem, smem, smem, smem],
            out_specs=(vmem, vmem),
            scratch_shapes=[
                pltpu.VMEM((n_dom, nb, ROWS, width), f32),
                pltpu.VMEM((slots, nb, ROWS, width), f32),
                pltpu.VMEM((slots, nb, width, nb * width), f32),
                pltpu.VMEM((nb, width, 3 * ROWS), jnp.bfloat16),
                pltpu.VMEM((nb, 3, width, width), f32),
                pltpu.VMEM((nb, 3, width, width), f32),
                pltpu.VMEM((nb, 3, width, width), f32),
                pltpu.VMEM((8, width), f32),
                pltpu.VMEM((slots, 8, width), f32),
                pltpu.VMEM((1, width), f32),
                pltpu.VMEM(((n_dom - 1) * (n_sub - 1), 1, width), f32),
                pltpu.VMEM((1, width), f32),
                pltpu.VMEM((n_dom * n_sub - 1, 1, width), f32),
                pltpu.SemaphoreType.DMA((slots,)),
                pltpu.SemaphoreType.DMA((slots,)),
                pltpu.SemaphoreType.DMA,
                pltpu.SemaphoreType.DMA,
                pltpu.SemaphoreType.DMA,
                pltpu.SemaphoreType.DMA,
                pltpu.SemaphoreType.DMA,
                pltpu.SemaphoreType.DMA,
            ],
            compiler_params=pltpu.CompilerParams(
                collective_id=0,
                has_side_effects=True,
                vmem_limit_bytes=4 * words + 8 * 1024 * 1024,
            ),
        )(
            segments,
            drag_coef,
            stress,
            send_ids.reshape(1, n_dom),
            partner_ids.reshape(1, n_dom),
        )

    in_specs = (
        P(("dom", "sub"), None, None),
        P(),
        P(("dom", "sub"), None),
        P(("dom", "sub"), None, None),
        P(("dom", "sub"), None, None),
    )
    out_specs = (P(("dom", "sub"), None, None), P(("dom", "sub"), None, None))
    return jax.shard_map(local, mesh=mesh, in_specs=in_specs, out_specs=out_specs, check_vma=False)
```

time: 171 us -> 26.9 us (0.16)
  blocking collectives: 87.8 us -> 0 us
  starting transfers between devices: 26.5 us -> 0 us
  other arithmetic: 25.6 us -> 0 us
  Pallas kernels: 0 us -> 24.1 us
  waiting for transfers between devices: 16.6 us -> 0 us
  local copies, waits for them, and re-layouts: 10 us -> 1.9 us
  between operations: 2.4 us -> 0.68 us
    pmax x2 -> x0, blocking collectives: 77 us -> none  [local(): top_sq = lax.pmax(jnp.max(speed_sq), ('dom', 'sub'))]
    all_to_all x5 -> x0, starting transfers between devices: 26.5 us -> none  [the longest x2 10.5 us: cross_forces(): lax.all_to_all(outgoing, 'dom', split_axis=0, concat_axis=0, tiled=True)]
    pallas_call x0 -> x1, Pallas kernels: none -> 24.1 us  [local(): pl.pallas_call(functools.partial(kernel, n_dom, n_sub), out_shape=(out, o...]
    reduce_sum x20 -> x0, other arithmetic: 17.2 us -> none  [force_on_target(): jnp.sum(weights * offset_c, axis=-1)]
    all_to_all x5 -> x0, waiting for transfers between devices: 16.6 us -> none  [the longest x2 10.8 us: cross_forces(): lax.all_to_all(going_back, 'dom', split_axis=0, concat_axis=0, tiled=True)]
    all_gather x2 -> x0, blocking collectives: 10.7 us -> none  [group_forces(): lax.all_gather(seg_state, 'sub', axis=0, tiled=True)]
    sub x3 -> x0, other arithmetic: 5.72 us -> none  [the longest x1 3.8 us: external_force(): first = pulled[1] * line_vec[:, 2] - pulled[2] * line_vec[:, 1]]
    slice x29 -> x0, local copies, waits for them, and re-layouts: 2.39 us -> none  [the longest x1 0.68 us: external_force(): stress[component, 0] * burgers[:, 0] + stress[component, 1] * burgers[:, 1]]
  transfers between devices with their start and end apart: 5 -> 0, of which waited for: 4 -> 0; matrix products, arithmetic and copies ran while one was open for 13% -> 0% of each run, Pallas kernels for 0% -> 0%
where the time goes in v1:
time: 26.9 us; the launch traced here: 26.7 us
  Pallas kernels  24.1 us (90%)
  local copies, waits for them, and re-layouts  1.9 us (7%)
  between operations  0.68 us (3%)
    pallas_call x1, Pallas kernels, local(): pl.pallas_call(functools.partial(kernel, n_dom, n_sub), out_shape=(out, o...  24.1 us
    pallas_call x2, local copies, waits for them, and re-layouts, local(): pl.pallas_call(functools.partial(kernel, n_dom, n_sub), out_shape=(out, o...  1.16 us
    unnamed x9, local copies, waits for them, and re-layouts  0.74 us

profile of v1, /device:TPU:0, one launch (start us, length us, event | category | flops | bytes accessed | tf_op | source)
XLA Modules:
  0.0 26.7 jit_solution(17030046059291340119)
XLA Ops:
  0.6 0.0 copy-start
  0.6 0.0 copy-start.1
  0.7 0.0 copy-start.2
  0.7 0.0 copy-start.3
  0.7 0.7 %copy.7.seg_ref = f32[2,9,128]{2,1,0:T(8,128)S(1)} copy(f32[2,9,128]{2,0,1:T(2,128)} %param.5) | data formatting | bytes 18432 | tf_op args[0]
  1.4 0.0 copy-done
  1.4 0.0 copy-done.1
  1.4 0.0 copy-done.2
  1.4 0.0 copy-done.3
  1.4 24.1 %shard_map.68 = (f32[2,3,128]{2,1,0:T(4,128)S(1)}, f32[2,3,128]{2,1,0:T(4,128)S(1)}) custom-call(f32[2,9,128]{2,1,0:T(8,128)S(1)} %copy.7.seg_ref, f32[2,128]{1,0:T(2,128)S(1)} %copy-done.1, f32[3,3]{1,0:T(4,128)S(1)} %copy-done, s32[1,8]{1,0:T(1,128)S(1)} %bitcast.2, s32[1,8]{1,0:T(1,128)S(1)} %bitcast.3), custom_call_target="tpu_custom_call" | custom-call | tf_op jit(solution)/shard_map/pallas_call | solution.py:357
  25.6 0.6 %copy.8 = f32[2,3,128]{2,0,1:T(2,128)} copy(f32[2,3,128]{2,1,0:T(4,128)S(1)} %get-tuple-element.2) | data formatting | bytes 6144 | tf_op jit(solution)/shard_map/pallas_call | solution.py:357
  26.2 0.6 %copy.9 = f32[2,3,128]{2,0,1:T(2,128)} copy(f32[2,3,128]{2,1,0:T(4,128)S(1)} %get-tuple-element.3) | data formatting | bytes 6144 | tf_op jit(solution)/shard_map/pallas_call | solution.py:357
Async XLA Ops:
  0.6 0.8 %copy-start = (f32[3,3]{1,0:T(4,128)S(1)}, f32[3,3]{1,0:T(4,128)}, u32[]{:S(2)}) copy-start(f32[3,3]{1,0:T(4,128)} %stress_ref.1) | copy-start | bytes 112
  0.6 0.8 %copy-start.1 = (f32[2,128]{1,0:T(2,128)S(1)}, f32[2,128]{1,0:T(2,128)}, u32[]{:S(2)}) copy-start(f32[2,128]{1,0:T(2,128)} %drag_ref.1) | copy-start | bytes 3076
  0.7 0.8 %copy-start.2 = (s32[1,8,1]{1,2,0:T(1,128)S(1)}, s32[1,8,1]{1,2,0:T(1,128)}, u32[]{:S(2)}) copy-start(s32[1,8,1]{1,2,0:T(1,128)} %param.8) | copy-start | bytes 100
  0.7 0.7 %copy-start.3 = (s32[1,8,1]{1,2,0:T(1,128)S(1)}, s32[1,8,1]{1,2,0:T(1,128)}, u32[]{:S(2)}) copy-start(s32[1,8,1]{1,2,0:T(1,128)} %param.9) | copy-start | bytes 100

commit v2 on v1

--- a/solution.py
+++ b/solution.py
@@ -15,8 +15,7 @@
 EPSILON = 1e-06
 
 MESH = pl.DeviceIdType.MESH
-ROWS = 16
-XROW, SROW, PROW = 9, 12, 13
+DEPTH = 80
 UNROLL_LIMIT = 64
 
 
@@ -87,23 +86,19 @@
     repeat(1, n_sub, greet_sub)
     repeat(1, n_dom, greet_dom)
 
-    products = []
+    used = 3 * nb
+    srow, prow, brow, lrow = used, used + 1, used + 2, 2 * used + 2
     for r in range(nb):
-        burgers = seg_ref[r, 6:9, :]
-        rows = [burgers[a : a + 1] * seg_ref[r, 3:6, :] for a in range(3)]
-        block = jnp.concatenate(rows + [jnp.zeros((ROWS - 9, width), jnp.float32)], axis=0)
-        products.append(block)
-        held[0, r] = block
-        held[0, r, XROW : XROW + 3, :] = seg_ref[r, 0:3, :]
-
-    whole = [held[0, r] for r in range(nb)]
-    row_id = lax.broadcasted_iota(jnp.int32, (ROWS, width), 0)
+        for first, source in ((0, 0), (brow, 6), (lrow, 3)):
+            held[0, first + 3 * r : first + 3 * r + 3, :] = seg_ref[r, source : source + 3, :]
+    held[0, srow : prow + 1, :] = jnp.zeros((2, width), jnp.float32)
+    whole = held[0]
+    row_id = lax.broadcasted_iota(jnp.int32, whole.shape, 0)
 
     def fill(q):
         sent = send_ref[0, q].astype(jnp.float32)
         partner = partner_ref[0, q].astype(jnp.float32)
-        for r in range(nb):
-            stage[q, r] = jnp.where(row_id == SROW, sent, jnp.where(row_id == PROW, partner, whole[r]))
+        stage[q] = jnp.where(row_id == srow, sent, jnp.where(row_id == prow, partner, whole))
 
     repeat(0, n_dom, fill)
 
@@ -150,6 +145,10 @@
     drag = jnp.concatenate(drag_rows + [zeros + 1.0], axis=0)
     position = jnp.concatenate([seg_ref[o, 0:3, :] for o in range(nb)] + [zeros], axis=0)
     lane = lax.broadcasted_iota(jnp.int32, (8, width), 1)
+    tile_row = lax.broadcasted_iota(jnp.int32, (8, width), 0)
+    diagonal = lax.broadcasted_iota(jnp.int32, (width, width), 0) == lax.broadcasted_iota(
+        jnp.int32, (width, width), 1
+    )
 
     def split(value):
         high = value.astype(jnp.bfloat16)
@@ -157,12 +156,15 @@
         return high, low
 
     for o in range(nb):
-        high = products[o].astype(jnp.bfloat16).astype(jnp.float32)
-        low = products[o] - high
-        left_side[o] = jnp.concatenate([high, high, low], axis=0).T.astype(jnp.bfloat16)
-        turned = whole[o].T
+        lines = jnp.concatenate([seg_ref[o, 3:6, :]] * nb + [zeros], axis=0)
+        product = jnp.concatenate([seg_ref[o, 6 + a : 7 + a, :] * lines for a in range(3)], axis=0)
+        high = product.astype(jnp.bfloat16).astype(jnp.float32)
+        rest = jnp.zeros((DEPTH - 72, width), jnp.float32)
+        left_side[o] = jnp.concatenate([high, high, product - high, rest], axis=0).T.astype(jnp.bfloat16)
+    turned = position.T
+    for o in range(nb):
         for c in range(3):
-            at_i[o, c] = jnp.broadcast_to(turned[:, XROW + c : XROW + c + 1], (width, width))
+            at_i[o, c] = jnp.broadcast_to(turned[:, 3 * o + c : 3 * o + c + 1], (width, width))
 
     def counts(slot, base, peer):
         table = []
@@ -176,7 +178,7 @@
                     value = value + jnp.where(mine, 1.0, 0.0)
                     source = stage if slot is None else held
                     place = dom if slot is None else slot
-                    got, for_mine = source[place, 0, SROW : SROW + 1, :], source[place, 0, PROW : PROW + 1, :]
+                    got, for_mine = source[place, srow : srow + 1, :], source[place, prow : prow + 1, :]
                     value = value + jnp.where(
                         jnp.logical_and(got == float(r), for_mine == float(o)), 1.0, 0.0
                     )
@@ -187,20 +189,27 @@
     def fill_numer(slot, base, peer):
         where = 0 if slot is None else slot
         table = counts(slot, base, peer)
+        lines = jnp.concatenate([held[where, lrow : lrow + used, :], zeros], axis=0)
+        pieces = []
+        for r in range(nb):
+            here = jnp.logical_and(tile_row >= 3 * r, tile_row < 3 * r + 3)
+            own_lines = jnp.where(here, lines, 0.0)
+            b = [held[where, brow + 3 * r + a : brow + 3 * r + a + 1, :] for a in range(3)]
+            pieces.append(jnp.concatenate([b[a] * own_lines for a in range(3)], axis=0))
         for o in range(nb):
-            right = jnp.concatenate([held[where, r] * table[o][r] for r in range(nb)], axis=1)
-            high, low = split(right)
+            right = jnp.concatenate([pieces[r] * table[o][r] for r in range(nb)], axis=1)
+            high = right.astype(jnp.bfloat16).astype(jnp.float32)
+            rest = jnp.zeros((DEPTH - 72, nb * width), jnp.float32)
+            stack = jnp.concatenate([high, right - high, high, rest], axis=0)
             numer[where, o] = jnp.dot(
-                left_side[o],
-                jnp.concatenate([high, low, high], axis=0),
-                preferred_element_type=jnp.float32,
+                left_side[o], stack.astype(jnp.bfloat16), preferred_element_type=jnp.float32
             )
 
     def add_slot(slot, step, first=False):
         rows = []
         for r in range(nb):
             for c in range(3):
-                row = held[slot, r, XROW + c : XROW + c + 1, :]
+                row = held[slot, 3 * r + c : 3 * r + c + 1, :]
                 if step is not None:
                     row = row + step * vel_rx[slot, r * 3 + c : r * 3 + c + 1, :]
                 rows.append(jnp.broadcast_to(row, (8, width)))
@@ -220,10 +229,15 @@
                     acc[o, c, part, :] = total[c]
 
     def velocity_of(position):
-        sums = []
-        for o in range(nb):
-            for c in range(3):
-                sums.append(jnp.sum(acc[o, c].T, axis=0, keepdims=True))
+        high, low = split(acc[...].reshape(used * width, width))
+        lane_sums = jnp.dot(
+            jnp.concatenate([high, low], axis=1),
+            jnp.ones((2 * width, width), jnp.bfloat16),
+            preferred_element_type=jnp.float32,
+        ).reshape(used, width, width)
+        sums = [
+            jnp.sum(jnp.where(diagonal, lane_sums[row], 0.0), axis=0, keepdims=True) for row in range(used)
+        ]
         pair = jnp.concatenate(sums + [zeros], axis=0)
         before = jnp.where(lane == 0, position, pltpu.roll(position, 1, 1))
         after = jnp.where(lane == width - 1, position, pltpu.roll(position, width - 1, 1))
@@ -353,17 +367,18 @@
         vmem = pl.BlockSpec(memory_space=pltpu.VMEM)
         smem = pl.BlockSpec(memory_space=pltpu.SMEM)
         out = jax.ShapeDtypeStruct((nb, 3, width), f32)
-        words = slots * nb * width * nb * width + (n_dom + slots) * nb * ROWS * width + 9 * nb * width * width
+        rows = 9 * nb + 2
+        words = slots * nb * width * nb * width + (n_dom + slots) * (rows + 8) * width + 9 * nb * width * width
         return pl.pallas_call(
             functools.partial(kernel, n_dom, n_sub),
             out_shape=(out, out),
             in_specs=[vmem, vmem, smem, smem, smem],
             out_specs=(vmem, vmem),
             scratch_shapes=[
-                pltpu.VMEM((n_dom, nb, ROWS, width), f32),
-                pltpu.VMEM((slots, nb, ROWS, width), f32),
+                pltpu.VMEM((n_dom, rows, width), f32),
+                pltpu.VMEM((slots, rows, width), f32),
                 pltpu.VMEM((slots, nb, width, nb * width), f32),
-                pltpu.VMEM((nb, width, 3 * ROWS), jnp.bfloat16),
+                pltpu.VMEM((nb, width, DEPTH), jnp.bfloat16),
                 pltpu.VMEM((nb, 3, width, width), f32),
                 pltpu.VMEM((nb, 3, width, width), f32),
                 pltpu.VMEM((nb, 3, width, width), f32),

time: 26.9 us -> 27.3 us (1.015)
  Pallas kernels: 24.1 us -> 24.5 us
    pallas_call x1, Pallas kernels: 24.1 us -> 24.5 us  [local(): pl.pallas_call(functools.partial(kernel, n_dom, n_sub), out_shape=(out, o...]
where the time goes in v2:
time: 27.3 us; the launch traced here: 27.1 us
  Pallas kernels  24.5 us (90%)
  local copies, waits for them, and re-layouts  1.9 us (7%)
  between operations  0.68 us (2%)
    pallas_call x1, Pallas kernels, local(): pl.pallas_call(functools.partial(kernel, n_dom, n_sub), out_shape=(out, o...  24.5 us
    pallas_call x2, local copies, waits for them, and re-layouts, local(): pl.pallas_call(functools.partial(kernel, n_dom, n_sub), out_shape=(out, o...  1.16 us
    unnamed x9, local copies, waits for them, and re-layouts  0.74 us

profile of v2, /device:TPU:0, one launch (start us, length us, event | category | flops | bytes accessed | tf_op | source)
XLA Modules:
  0.0 27.1 jit_solution(16022447557758305380)
XLA Ops:
  0.6 0.0 copy-start
  0.6 0.0 copy-start.1
  0.7 0.0 copy-start.2
  0.7 0.0 copy-start.3
  0.7 0.7 %copy.7.seg_ref = f32[2,9,128]{2,1,0:T(8,128)S(1)} copy(f32[2,9,128]{2,0,1:T(2,128)} %param.5) | data formatting | bytes 18432 | tf_op args[0]
  1.4 0.0 copy-done
  1.4 0.0 copy-done.1
  1.4 0.0 copy-done.2
  1.4 0.0 copy-done.3
  1.4 24.5 %shard_map.68 = (f32[2,3,128]{2,1,0:T(4,128)S(1)}, f32[2,3,128]{2,1,0:T(4,128)S(1)}) custom-call(f32[2,9,128]{2,1,0:T(8,128)S(1)} %copy.7.seg_ref, f32[2,128]{1,0:T(2,128)S(1)} %copy-done.1, f32[3,3]{1,0:T(4,128)S(1)} %copy-done, s32[1,8]{1,0:T(1,128)S(1)} %bitcast.2, s32[1,8]{1,0:T(1,128)S(1)} %bitcast.3), custom_call_target="tpu_custom_call" | custom-call | tf_op jit(solution)/shard_map/pallas_call | solution.py:372
  25.9 0.6 %copy.8 = f32[2,3,128]{2,0,1:T(2,128)} copy(f32[2,3,128]{2,1,0:T(4,128)S(1)} %get-tuple-element.2) | data formatting | bytes 6144 | tf_op jit(solution)/shard_map/pallas_call | solution.py:372
  26.5 0.6 %copy.9 = f32[2,3,128]{2,0,1:T(2,128)} copy(f32[2,3,128]{2,1,0:T(4,128)S(1)} %get-tuple-element.3) | data formatting | bytes 6144 | tf_op jit(solution)/shard_map/pallas_call | solution.py:372
Async XLA Ops:
  0.6 0.8 %copy-start = (f32[3,3]{1,0:T(4,128)S(1)}, f32[3,3]{1,0:T(4,128)}, u32[]{:S(2)}) copy-start(f32[3,3]{1,0:T(4,128)} %stress_ref.1) | copy-start | bytes 112
  0.6 0.8 %copy-start.1 = (f32[2,128]{1,0:T(2,128)S(1)}, f32[2,128]{1,0:T(2,128)}, u32[]{:S(2)}) copy-start(f32[2,128]{1,0:T(2,128)} %drag_ref.1) | copy-start | bytes 3076
  0.7 0.8 %copy-start.2 = (s32[1,8,1]{1,2,0:T(1,128)S(1)}, s32[1,8,1]{1,2,0:T(1,128)}, u32[]{:S(2)}) copy-start(s32[1,8,1]{1,2,0:T(1,128)} %param.8) | copy-start | bytes 100
  0.7 0.7 %copy-start.3 = (s32[1,8,1]{1,2,0:T(1,128)S(1)}, s32[1,8,1]{1,2,0:T(1,128)}, u32[]{:S(2)}) copy-start(s32[1,8,1]{1,2,0:T(1,128)} %param.9) | copy-start | bytes 100

commit v3 on v2

--- a/solution.py
+++ b/solution.py
@@ -51,18 +51,14 @@
     acc,
     vel_tx,
     vel_rx,
-    top1_tx,
-    top1_rx,
-    top2_tx,
-    top2_rx,
+    top_tx,
+    top_rx,
     state_send,
     state_recv,
     vel_send,
     vel_recv,
-    top1_send,
-    top1_recv,
-    top2_send,
-    top2_recv,
+    top_send,
+    top_recv,
 ):
     nb, _, width = seg_ref.shape
     slots = n_sub + n_dom - 1
@@ -91,9 +87,10 @@
     for r in range(nb):
         for first, source in ((0, 0), (brow, 6), (lrow, 3)):
             held[0, first + 3 * r : first + 3 * r + 3, :] = seg_ref[r, source : source + 3, :]
-    held[0, srow : prow + 1, :] = jnp.zeros((2, width), jnp.float32)
+    held[0, srow : prow + 1, :] = jnp.full((2, width), -1.0, jnp.float32)
     whole = held[0]
     row_id = lax.broadcasted_iota(jnp.int32, whole.shape, 0)
+    stage[n_dom] = whole
 
     def fill(q):
         sent = send_ref[0, q].astype(jnp.float32)
@@ -101,10 +98,11 @@
         stage[q] = jnp.where(row_id == srow, sent, jnp.where(row_id == prow, partner, whole))
 
     repeat(0, n_dom, fill)
+    held[0] = stage[dom]
 
     def sub_copy(k):
         return pltpu.make_async_remote_copy(
-            src_ref=held.at[0],
+            src_ref=stage.at[n_dom],
             dst_ref=held.at[k],
             send_sem=state_send.at[k],
             recv_sem=state_recv.at[k],
@@ -166,29 +164,22 @@
         for c in range(3):
             at_i[o, c] = jnp.broadcast_to(turned[:, 3 * o + c : 3 * o + c + 1], (width, width))
 
-    def counts(slot, base, peer):
+    def fill_numer(where):
+        base = jnp.full((1, width), jnp.where(where < n_sub, 1.0, 0.0), jnp.float32)
+        in_column = where >= n_sub
+        peer = jnp.where(in_column, lax.rem(dom - where + n_sub - 1 + n_dom, n_dom), dom)
+        listed = jnp.logical_or(in_column, where == 0)
+        sent = jnp.where(listed, send_ref[0, peer], -1)
+        partner = partner_ref[0, peer]
+        got, for_mine = held[where, srow : srow + 1, :], held[where, prow : prow + 1, :]
         table = []
         for o in range(nb):
             row = []
             for r in range(nb):
-                value = jnp.full((1, width), base, jnp.float32)
-                if peer is not None:
-                    sent, partner = send_ref[0, peer], partner_ref[0, peer]
-                    mine = jnp.logical_and(sent == o, partner == r)
-                    value = value + jnp.where(mine, 1.0, 0.0)
-                    source = stage if slot is None else held
-                    place = dom if slot is None else slot
-                    got, for_mine = source[place, srow : srow + 1, :], source[place, prow : prow + 1, :]
-                    value = value + jnp.where(
-                        jnp.logical_and(got == float(r), for_mine == float(o)), 1.0, 0.0
-                    )
-                row.append(value)
+                mine = jnp.logical_and(sent == o, partner == r)
+                theirs = jnp.logical_and(got == float(r), for_mine == float(o))
+                row.append(base + jnp.where(mine, 1.0, 0.0) + jnp.where(theirs, 1.0, 0.0))
             table.append(row)
-        return table
-
-    def fill_numer(slot, base, peer):
-        where = 0 if slot is None else slot
-        table = counts(slot, base, peer)
         lines = jnp.concatenate([held[where, lrow : lrow + used, :], zeros], axis=0)
         pieces = []
         for r in range(nb):
@@ -205,26 +196,24 @@
                 left_side[o], stack.astype(jnp.bfloat16), preferred_element_type=jnp.float32
             )
 
-    def add_slot(slot, step, first=False):
+    def add_slot(slot):
         rows = []
         for r in range(nb):
             for c in range(3):
                 row = held[slot, 3 * r + c : 3 * r + c + 1, :]
-                if step is not None:
-                    row = row + step * vel_rx[slot, r * 3 + c : r * 3 + c + 1, :]
                 rows.append(jnp.broadcast_to(row, (8, width)))
         for o in range(nb):
             for g in range(width // 8):
                 part = pl.ds(8 * g, 8)
                 mine = [at_i[o, c, part, :] for c in range(3)]
-                total = None if first else [acc[o, c, part, :] for c in range(3)]
+                total = [acc[o, c, part, :] for c in range(3)]
                 for r in range(nb):
                     off = [mine[c] - rows[r * 3 + c] for c in range(3)]
                     square = CORE_SQUARE + off[0] * off[0] + off[1] * off[1] + off[2] * off[2]
                     inverse = lax.rsqrt(square)
                     weight = numer[slot, o, part, pl.ds(width * r, width)] * inverse * (inverse * inverse)
                     terms = [weight * off[c] for c in range(3)]
-                    total = terms if total is None else [total[c] + terms[c] for c in range(3)]
+                    total = [total[c] + terms[c] for c in range(3)]
                 for c in range(3):
                     acc[o, c, part, :] = total[c]
 
@@ -254,107 +243,89 @@
         top = jnp.max(row, axis=1, keepdims=True)
         return STEP_LENGTH / (jnp.sqrt(top) + EPSILON)
 
-    fill_numer(None, 1.0, dom)
-    add_slot(0, None, first=True)
-
-    def from_sub(k, carry):
-        sub_copy(k).wait_recv()
-        fill_numer(k, 1.0, None)
-        add_slot(k, None)
-        return carry
-
-    def from_dom(k, carry):
-        slot = n_sub - 1 + k
-        dom_copy(k).wait_recv()
-        fill_numer(slot, 0.0, lax.rem(dom - k + n_dom, n_dom))
-        add_slot(slot, None)
-        return carry
-
-    lax.fori_loop(1, n_sub, from_sub, 0)
-    lax.fori_loop(1, n_dom, from_dom, 0)
-    velocity, top = velocity_of(position)
-    vel_tx[...] = jnp.concatenate([velocity[0 : 3 * nb], top, zeros[: spare - 1]], axis=0)
-    top1_tx[...] = top
-
-    def vel_copy(slot, target):
+    def vel_copy(slot, device):
         return pltpu.make_async_remote_copy(
             src_ref=vel_tx,
             dst_ref=vel_rx.at[slot],
             send_sem=vel_send,
             recv_sem=vel_recv,
-            device_id=target,
+            device_id=device,
             device_id_type=MESH,
         )
 
-    def top1_copy(index):
-        kd, ks = index // (n_sub - 1) + 1, index % (n_sub - 1) + 1
-        return pltpu.make_async_remote_copy(
-            src_ref=top1_tx,
-            dst_ref=top1_rx.at[index],
-            send_sem=top1_send,
-            recv_sem=top1_recv,
-            device_id=(lax.rem(dom + kd, n_dom), lax.rem(sub + ks, n_sub)),
-            device_id_type=MESH,
-        )
-
-    others = (n_sub - 1) * (n_dom - 1)
-    repeat(1, n_dom, lambda k: vel_copy(n_sub - 1 + k, dom_at(k)).start())
-    repeat(0, others, lambda k: top1_copy(k).start())
-    repeat(1, n_sub, lambda k: vel_copy(k, sub_at(k)).start())
-
-    vel_rx[0] = vel_tx[...]
-    turned = velocity.T
-    for o in range(nb):
-        for c in range(3):
-            vel_i[o, c] = jnp.broadcast_to(turned[:, 3 * o + c : 3 * o + c + 1], (width, width))
-
     arrived = vel_rx.at[pl.ds(1, slots - 1)]
-    pltpu.make_async_copy(arrived, arrived, vel_recv).wait()
-    pltpu.make_async_copy(top1_rx, top1_rx, top1_recv).wait()
-    near = jnp.max(vel_rx[:, 3 * nb : 3 * nb + 1, :], axis=0)
-    far = jnp.max(top1_rx[...], axis=0)
-    step = step_length(jnp.maximum(near, far))
-
-    position = position + step * velocity
-    for o in range(nb):
-        for c in range(3):
-            at_i[o, c] = at_i[o, c] + step * vel_i[o, c]
-    add_slot(0, step, first=True)
-
-    def again(slot, carry):
-        add_slot(slot, carry)
-        return carry
-
-    lax.fori_loop(1, slots, again, step)
-    velocity, top = velocity_of(position)
-    top2_tx[...] = top
-
-    def top2_copy(index):
-        kd, ks = (index + 1) // n_sub, (index + 1) % n_sub
-        return pltpu.make_async_remote_copy(
-            src_ref=top2_tx,
-            dst_ref=top2_rx.at[index],
-            send_sem=top2_send,
-            recv_sem=top2_recv,
-            device_id=(lax.rem(dom + kd, n_dom), lax.rem(sub + ks, n_sub)),
-            device_id_type=MESH,
-        )
-
-    repeat(0, n_sub * n_dom - 1, lambda k: top2_copy(k).start())
+
+    def one_step(index, carry):
+        position, _ = carry
+        acc[...] = jnp.zeros_like(acc)
+
+        def one_slot(slot, inner):
+            @pl.when(index == 0)
+            def _():
+                @pl.when(slot > 0)
+                def _():
+                    arrival = held.at[slot]
+                    pltpu.make_async_copy(arrival, arrival, state_recv.at[slot]).wait()
+
+                fill_numer(slot)
+
+            add_slot(slot)
+            return inner
+
+        lax.fori_loop(0, slots, one_slot, 0)
+        velocity, top = velocity_of(position)
+        top_tx[index] = top
+
+        def top_copy(place):
+            kd, ks = (place + 1) // n_sub, (place + 1) % n_sub
+            return pltpu.make_async_remote_copy(
+                src_ref=top_tx.at[index],
+                dst_ref=top_rx.at[index, place],
+                send_sem=top_send.at[index],
+                recv_sem=top_recv.at[index],
+                device_id=(lax.rem(dom + kd, n_dom), lax.rem(sub + ks, n_sub)),
+                device_id_type=MESH,
+            )
+
+        @pl.when(index == 0)
+        def _():
+            vel_tx[...] = velocity
+            repeat(1, n_dom, lambda k: vel_copy(n_sub - 1 + k, dom_at(k)).start())
+            repeat(1, n_sub, lambda k: vel_copy(k, sub_at(k)).start())
+
+        repeat(0, n_sub * n_dom - 1, lambda k: top_copy(k).start())
+
+        @pl.when(index == 0)
+        def _():
+            vel_rx[0] = velocity
+            turned = velocity.T
+            for o in range(nb):
+                for c in range(3):
+                    vel_i[o, c] = jnp.broadcast_to(turned[:, 3 * o + c : 3 * o + c + 1], (width, width))
+            pltpu.make_async_copy(arrived, arrived, vel_recv).wait()
+
+        tops = top_rx.at[index]
+        pltpu.make_async_copy(tops, tops, top_recv.at[index]).wait()
+        step = step_length(jnp.maximum(jnp.max(top_rx[index], axis=0), top))
+
+        @pl.when(index == 0)
+        def _():
+            at_i[...] = at_i[...] + step * vel_i[...]
+            held[:, 0:8, :] = held[:, 0:8, :] + step * vel_rx[...]
+
+        return position + step * velocity, velocity
+
+    position, velocity = lax.fori_loop(0, STEPS, one_step, (position, jnp.zeros_like(position)))
     for o in range(nb):
         vel_ref[o] = velocity[3 * o : 3 * o + 3]
+        pos_ref[o] = position[3 * o : 3 * o + 3]
 
     repeat(1, n_sub, lambda k: sub_copy(k).wait_send())
     repeat(1, n_dom, lambda k: dom_copy(k).wait_send())
     pltpu.make_async_copy(arrived, arrived, vel_send).wait()
-    pltpu.make_async_copy(top1_rx, top1_rx, top1_send).wait()
-
-    pltpu.make_async_copy(top2_rx, top2_rx, top2_recv).wait()
-    step = step_length(jnp.maximum(jnp.max(top2_rx[...], axis=0), top))
-    position = position + step * velocity
-    for o in range(nb):
-        pos_ref[o] = position[3 * o : 3 * o + 3]
-    pltpu.make_async_copy(top2_rx, top2_rx, top2_send).wait()
+    for index in range(STEPS):
+        tops = top_rx.at[index]
+        pltpu.make_async_copy(tops, tops, top_send.at[index]).wait()
 
 
 def solution(mesh):
@@ -368,14 +339,14 @@
         smem = pl.BlockSpec(memory_space=pltpu.SMEM)
         out = jax.ShapeDtypeStruct((nb, 3, width), f32)
         rows = 9 * nb + 2
-        words = slots * nb * width * nb * width + (n_dom + slots) * (rows + 8) * width + 9 * nb * width * width
+        words = 2 * STEPS * n_dom * n_sub * width + slots * nb * width * nb * width + (n_dom + slots) * (rows + 8) * width + 9 * nb * width * width
         return pl.pallas_call(
             functools.partial(kernel, n_dom, n_sub),
             out_shape=(out, out),
             in_specs=[vmem, vmem, smem, smem, smem],
             out_specs=(vmem, vmem),
             scratch_shapes=[
-                pltpu.VMEM((n_dom, rows, width), f32),
+                pltpu.VMEM((n_dom + 1, rows, width), f32),
                 pltpu.VMEM((slots, rows, width), f32),
                 pltpu.VMEM((slots, nb, width, nb * width), f32),
                 pltpu.VMEM((nb, width, DEPTH), jnp.bfloat16),
@@ -384,18 +355,14 @@
                 pltpu.VMEM((nb, 3, width, width), f32),
                 pltpu.VMEM((8, width), f32),
                 pltpu.VMEM((slots, 8, width), f32),
-                pltpu.VMEM((1, width), f32),
-                pltpu.VMEM(((n_dom - 1) * (n_sub - 1), 1, width), f32),
-                pltpu.VMEM((1, width), f32),
-                pltpu.VMEM((n_dom * n_sub - 1, 1, width), f32),
+                pltpu.VMEM((STEPS, 1, width), f32),
+                pltpu.VMEM((STEPS, n_dom * n_sub - 1, 1, width), f32),
                 pltpu.SemaphoreType.DMA((slots,)),
                 pltpu.SemaphoreType.DMA((slots,)),
                 pltpu.SemaphoreType.DMA,
                 pltpu.SemaphoreType.DMA,
-                pltpu.SemaphoreType.DMA,
-                pltpu.SemaphoreType.DMA,
-                pltpu.SemaphoreType.DMA,
-                pltpu.SemaphoreType.DMA,
+                pltpu.SemaphoreType.DMA((STEPS,)),
+                pltpu.SemaphoreType.DMA((STEPS,)),
             ],
             compiler_params=pltpu.CompilerParams(
                 collective_id=0,

time: 27.3 us -> 27.9 us (1.022)
  Pallas kernels: 24.5 us -> 25.1 us
    pallas_call x1, Pallas kernels: 24.5 us -> 25.1 us  [local(): pl.pallas_call(functools.partial(kernel, n_dom, n_sub), out_shape=(out, o...]
where the time goes in v3:
time: 27.9 us; the launch traced here: 27.7 us
  Pallas kernels  25.1 us (90%)
  local copies, waits for them, and re-layouts  1.9 us (7%)
  between operations  0.68 us (2%)
    pallas_call x1, Pallas kernels, local(): pl.pallas_call(functools.partial(kernel, n_dom, n_sub), out_shape=(out, o...  25.1 us
    pallas_call x2, local copies, waits for them, and re-layouts, local(): pl.pallas_call(functools.partial(kernel, n_dom, n_sub), out_shape=(out, o...  1.16 us
    unnamed x9, local copies, waits for them, and re-layouts  0.74 us

profile of v3, /device:TPU:0, one launch (start us, length us, event | category | flops | bytes accessed | tf_op | source)
XLA Modules:
  0.0 27.7 jit_solution(7425462989732391790)
XLA Ops:
  0.6 0.0 copy-start
  0.6 0.0 copy-start.1
  0.7 0.0 copy-start.2
  0.7 0.0 copy-start.3
  0.7 0.7 %copy.7.seg_ref = f32[2,9,128]{2,1,0:T(8,128)S(1)} copy(f32[2,9,128]{2,0,1:T(2,128)} %param.5) | data formatting | bytes 18432 | tf_op args[0]
  1.4 0.0 copy-done
  1.4 0.0 copy-done.1
  1.4 0.0 copy-done.2
  1.4 0.0 copy-done.3
  1.4 25.1 %shard_map.68 = (f32[2,3,128]{2,1,0:T(4,128)S(1)}, f32[2,3,128]{2,1,0:T(4,128)S(1)}) custom-call(f32[2,9,128]{2,1,0:T(8,128)S(1)} %copy.7.seg_ref, f32[2,128]{1,0:T(2,128)S(1)} %copy-done.1, f32[3,3]{1,0:T(4,128)S(1)} %copy-done, s32[1,8]{1,0:T(1,128)S(1)} %bitcast.2, s32[1,8]{1,0:T(1,128)S(1)} %bitcast.3), custom_call_target="tpu_custom_call" | custom-call | tf_op jit(solution)/shard_map/pallas_call | solution.py:343
  26.5 0.6 %copy.8 = f32[2,3,128]{2,0,1:T(2,128)} copy(f32[2,3,128]{2,1,0:T(4,128)S(1)} %get-tuple-element.2) | data formatting | bytes 6144 | tf_op jit(solution)/shard_map/pallas_call | solution.py:343
  27.1 0.6 %copy.9 = f32[2,3,128]{2,0,1:T(2,128)} copy(f32[2,3,128]{2,1,0:T(4,128)S(1)} %get-tuple-element.3) | data formatting | bytes 6144 | tf_op jit(solution)/shard_map/pallas_call | solution.py:343
Async XLA Ops:
  0.6 0.8 %copy-start = (f32[3,3]{1,0:T(4,128)S(1)}, f32[3,3]{1,0:T(4,128)}, u32[]{:S(2)}) copy-start(f32[3,3]{1,0:T(4,128)} %stress_ref.1) | copy-start | bytes 112
  0.6 0.8 %copy-start.1 = (f32[2,128]{1,0:T(2,128)S(1)}, f32[2,128]{1,0:T(2,128)}, u32[]{:S(2)}) copy-start(f32[2,128]{1,0:T(2,128)} %drag_ref.1) | copy-start | bytes 3076
  0.7 0.8 %copy-start.2 = (s32[1,8,1]{1,2,0:T(1,128)S(1)}, s32[1,8,1]{1,2,0:T(1,128)}, u32[]{:S(2)}) copy-start(s32[1,8,1]{1,2,0:T(1,128)} %param.8) | copy-start | bytes 100
  0.7 0.7 %copy-start.3 = (s32[1,8,1]{1,2,0:T(1,128)S(1)}, s32[1,8,1]{1,2,0:T(1,128)}, u32[]{:S(2)}) copy-start(s32[1,8,1]{1,2,0:T(1,128)} %param.9) | copy-start | bytes 100

commit v4 on v2

--- a/solution.py
+++ b/solution.py
@@ -49,6 +49,7 @@
     at_i,
     vel_i,
     acc,
+    sources,
     vel_tx,
     vel_rx,
     top1_tx,
@@ -316,16 +317,43 @@
     step = step_length(jnp.maximum(near, far))
 
     position = position + step * velocity
-    for o in range(nb):
-        for c in range(3):
-            at_i[o, c] = at_i[o, c] + step * vel_i[o, c]
-    add_slot(0, step, first=True)
-
-    def again(slot, carry):
-        add_slot(slot, carry)
+
+    def move(slot):
+        tile = held[slot, 0:8, :] + step * vel_rx[slot]
+        for row in range(used):
+            sources[slot, row] = jnp.broadcast_to(tile[row : row + 1], (8, width))
+
+    repeat(0, slots, move)
+
+    def chunk(g, carry):
+        part = pl.ds(pl.multiple_of(8 * g, 8), 8)
+        mine = [[at_i[o, c, part, :] + step * vel_i[o, c, part, :] for c in range(3)] for o in range(nb)]
+
+        def add_one(slot, total):
+            total = list(total)
+            for r in range(nb):
+                theirs = [sources[slot, 3 * r + c] for c in range(3)]
+                for o in range(nb):
+                    off = [mine[o][c] - theirs[c] for c in range(3)]
+                    square = CORE_SQUARE + off[0] * off[0] + off[1] * off[1] + off[2] * off[2]
+                    inverse = lax.rsqrt(square)
+                    weight = numer[slot, o, part, pl.ds(width * r, width)] * inverse * (inverse * inverse)
+                    for c in range(3):
+                        total[3 * o + c] = total[3 * o + c] + weight * off[c]
+            return total
+
+        total = [jnp.zeros((8, width), jnp.float32)] * used
+        if slots <= UNROLL_LIMIT:
+            for slot in range(slots):
+                total = add_one(slot, total)
+        else:
+            total = lax.fori_loop(0, slots, add_one, total)
+        for o in range(nb):
+            for c in range(3):
+                acc[o, c, part, :] = total[3 * o + c]
         return carry
 
-    lax.fori_loop(1, slots, again, step)
+    lax.fori_loop(0, width // 8, chunk, 0, unroll=4)
     velocity, top = velocity_of(position)
     top2_tx[...] = top
 
@@ -368,7 +396,7 @@
         smem = pl.BlockSpec(memory_space=pltpu.SMEM)
         out = jax.ShapeDtypeStruct((nb, 3, width), f32)
         rows = 9 * nb + 2
-        words = slots * nb * width * nb * width + (n_dom + slots) * (rows + 8) * width + 9 * nb * width * width
+        words = 48 * slots * width + slots * nb * width * nb * width + (n_dom + slots) * (rows + 8) * width + 9 * nb * width * width
         return pl.pallas_call(
             functools.partial(kernel, n_dom, n_sub),
             out_shape=(out, out),
@@ -382,6 +410,7 @@
                 pltpu.VMEM((nb, 3, width, width), f32),
                 pltpu.VMEM((nb, 3, width, width), f32),
                 pltpu.VMEM((nb, 3, width, width), f32),
+                pltpu.VMEM((slots, 3 * nb, 8, width), f32),
                 pltpu.VMEM((8, width), f32),
                 pltpu.VMEM((slots, 8, width), f32),
                 pltpu.VMEM((1, width), f32),

time: 27.3 us -> 27 us (0.989)
  no operation moved by 1% of the time
where the time goes in v4:
time: 27 us; the launch traced here: 26.9 us
  Pallas kernels  24.3 us (90%)
  local copies, waits for them, and re-layouts  1.9 us (7%)
  between operations  0.68 us (3%)
    pallas_call x1, Pallas kernels, local(): pl.pallas_call(functools.partial(kernel, n_dom, n_sub), out_shape=(out, o...  24.3 us
    pallas_call x2, local copies, waits for them, and re-layouts, local(): pl.pallas_call(functools.partial(kernel, n_dom, n_sub), out_shape=(out, o...  1.16 us
    unnamed x9, local copies, waits for them, and re-layouts  0.74 us

profile of v4, /device:TPU:0, one launch (start us, length us, event | category | flops | bytes accessed | tf_op | source)
XLA Modules:
  0.0 26.9 jit_solution(15975370817786531591)
XLA Ops:
  0.6 0.0 copy-start
  0.6 0.0 copy-start.1
  0.7 0.0 copy-start.2
  0.7 0.0 copy-start.3
  0.7 0.7 %copy.7.seg_ref = f32[2,9,128]{2,1,0:T(8,128)S(1)} copy(f32[2,9,128]{2,0,1:T(2,128)} %param.5) | data formatting | bytes 18432 | tf_op args[0]
  1.4 0.0 copy-done
  1.4 0.0 copy-done.1
  1.4 0.0 copy-done.2
  1.4 0.0 copy-done.3
  1.4 24.3 %shard_map.68 = (f32[2,3,128]{2,1,0:T(4,128)S(1)}, f32[2,3,128]{2,1,0:T(4,128)S(1)}) custom-call(f32[2,9,128]{2,1,0:T(8,128)S(1)} %copy.7.seg_ref, f32[2,128]{1,0:T(2,128)S(1)} %copy-done.1, f32[3,3]{1,0:T(4,128)S(1)} %copy-done, s32[1,8]{1,0:T(1,128)S(1)} %bitcast.2, s32[1,8]{1,0:T(1,128)S(1)} %bitcast.3), custom_call_target="tpu_custom_call" | custom-call | tf_op jit(solution)/shard_map/pallas_call | solution.py:400
  25.7 0.6 %copy.8 = f32[2,3,128]{2,0,1:T(2,128)} copy(f32[2,3,128]{2,1,0:T(4,128)S(1)} %get-tuple-element.2) | data formatting | bytes 6144 | tf_op jit(solution)/shard_map/pallas_call | solution.py:400
  26.3 0.6 %copy.9 = f32[2,3,128]{2,0,1:T(2,128)} copy(f32[2,3,128]{2,1,0:T(4,128)S(1)} %get-tuple-element.3) | data formatting | bytes 6144 | tf_op jit(solution)/shard_map/pallas_call | solution.py:400
Async XLA Ops:
  0.6 0.8 %copy-start = (f32[3,3]{1,0:T(4,128)S(1)}, f32[3,3]{1,0:T(4,128)}, u32[]{:S(2)}) copy-start(f32[3,3]{1,0:T(4,128)} %stress_ref.1) | copy-start | bytes 112
  0.6 0.8 %copy-start.1 = (f32[2,128]{1,0:T(2,128)S(1)}, f32[2,128]{1,0:T(2,128)}, u32[]{:S(2)}) copy-start(f32[2,128]{1,0:T(2,128)} %drag_ref.1) | copy-start | bytes 3076
  0.7 0.8 %copy-start.2 = (s32[1,8,1]{1,2,0:T(1,128)S(1)}, s32[1,8,1]{1,2,0:T(1,128)}, u32[]{:S(2)}) copy-start(s32[1,8,1]{1,2,0:T(1,128)} %param.8) | copy-start | bytes 100
  0.7 0.7 %copy-start.3 = (s32[1,8,1]{1,2,0:T(1,128)S(1)}, s32[1,8,1]{1,2,0:T(1,128)}, u32[]{:S(2)}) copy-start(s32[1,8,1]{1,2,0:T(1,128)} %param.9) | copy-start | bytes 100

commit v5 on v4

--- a/solution.py
+++ b/solution.py
@@ -124,10 +124,6 @@
             device_id_type=MESH,
         )
 
-    pl.semaphore_wait(barrier, slots - 1)
-    repeat(1, n_dom, lambda k: dom_copy(k).start())
-    repeat(1, n_sub, lambda k: sub_copy(k).start())
-
     applied_rows = []
     drag_rows = []
     for o in range(nb):
@@ -257,6 +253,10 @@
 
     fill_numer(None, 1.0, dom)
     add_slot(0, None, first=True)
+
+    pl.semaphore_wait(barrier, slots - 1)
+    repeat(1, n_dom, lambda k: dom_copy(k).start())
+    repeat(1, n_sub, lambda k: sub_copy(k).start())
 
     def from_sub(k, carry):
         sub_copy(k).wait_recv()

time: 27 us -> 27 us (level)
  no operation moved by 1% of the time
where the time goes in v5:
time: 27 us; the launch traced here: 26.8 us
  Pallas kernels  24.3 us (90%)
  local copies, waits for them, and re-layouts  1.9 us (7%)
  between operations  0.68 us (3%)
    pallas_call x1, Pallas kernels, local(): pl.pallas_call(functools.partial(kernel, n_dom, n_sub), out_shape=(out, o...  24.3 us
    pallas_call x2, local copies, waits for them, and re-layouts, local(): pl.pallas_call(functools.partial(kernel, n_dom, n_sub), out_shape=(out, o...  1.16 us
    unnamed x9, local copies, waits for them, and re-layouts  0.74 us

profile of v5, /device:TPU:0, one launch (start us, length us, event | category | flops | bytes accessed | tf_op | source)
XLA Modules:
  0.0 26.8 jit_solution(13810448255968380371)
XLA Ops:
  0.6 0.0 copy-start
  0.6 0.0 copy-start.1
  0.7 0.0 copy-start.2
  0.7 0.0 copy-start.3
  0.7 0.7 %copy.7.seg_ref = f32[2,9,128]{2,1,0:T(8,128)S(1)} copy(f32[2,9,128]{2,0,1:T(2,128)} %param.5) | data formatting | bytes 18432 | tf_op args[0]
  1.4 0.0 copy-done
  1.4 0.0 copy-done.1
  1.4 0.0 copy-done.2
  1.4 0.0 copy-done.3
  1.4 24.3 %shard_map.68 = (f32[2,3,128]{2,1,0:T(4,128)S(1)}, f32[2,3,128]{2,1,0:T(4,128)S(1)}) custom-call(f32[2,9,128]{2,1,0:T(8,128)S(1)} %copy.7.seg_ref, f32[2,128]{1,0:T(2,128)S(1)} %copy-done.1, f32[3,3]{1,0:T(4,128)S(1)} %copy-done, s32[1,8]{1,0:T(1,128)S(1)} %bitcast.2, s32[1,8]{1,0:T(1,128)S(1)} %bitcast.3), custom_call_target="tpu_custom_call" | custom-call | tf_op jit(solution)/shard_map/pallas_call | solution.py:400
  25.7 0.6 %copy.8 = f32[2,3,128]{2,0,1:T(2,128)} copy(f32[2,3,128]{2,1,0:T(4,128)S(1)} %get-tuple-element.2) | data formatting | bytes 6144 | tf_op jit(solution)/shard_map/pallas_call | solution.py:400
  26.3 0.6 %copy.9 = f32[2,3,128]{2,0,1:T(2,128)} copy(f32[2,3,128]{2,1,0:T(4,128)S(1)} %get-tuple-element.3) | data formatting | bytes 6144 | tf_op jit(solution)/shard_map/pallas_call | solution.py:400
Async XLA Ops:
  0.6 0.8 %copy-start = (f32[3,3]{1,0:T(4,128)S(1)}, f32[3,3]{1,0:T(4,128)}, u32[]{:S(2)}) copy-start(f32[3,3]{1,0:T(4,128)} %stress_ref.1) | copy-start | bytes 112
  0.6 0.8 %copy-start.1 = (f32[2,128]{1,0:T(2,128)S(1)}, f32[2,128]{1,0:T(2,128)}, u32[]{:S(2)}) copy-start(f32[2,128]{1,0:T(2,128)} %drag_ref.1) | copy-start | bytes 3076
  0.7 0.8 %copy-start.2 = (s32[1,8,1]{1,2,0:T(1,128)S(1)}, s32[1,8,1]{1,2,0:T(1,128)}, u32[]{:S(2)}) copy-start(s32[1,8,1]{1,2,0:T(1,128)} %param.8) | copy-start | bytes 100
  0.7 0.7 %copy-start.3 = (s32[1,8,1]{1,2,0:T(1,128)S(1)}, s32[1,8,1]{1,2,0:T(1,128)}, u32[]{:S(2)}) copy-start(s32[1,8,1]{1,2,0:T(1,128)} %param.9) | copy-start | bytes 100
